TPU v7x, 32 devices: a whole 2x2x4 slice. The times are simulated.
32 devices in a mesh: stream: 8 (over z, y), pitch: 4 (over x, core).
Axes of the slice: x: 2, y: 2, z: 4, core: 2. Of those that a mesh axis runs over, the one named last changes fastest.
Arguments:
- velocity: float32 [64, 64, 1024], P('stream', 'pitch'), may hold values from -6 to 6
- eddy_visc: float32 [64, 64, 1024], P('stream', 'pitch'), may hold values from 0.02 to 0.3
- stream_op: float32 [64, 64], replicated, may hold values from -0.75 to 0.75
- inlet_col: float32 [64], replicated, may hold values from -5 to 5
- planes: float32 [8, 64, 1024], P('stream', 'pitch'), may hold values from -6 to 6
- record: int32 [4], replicated, may hold values from 0 to 7
- convection: float32 [64], P('pitch'), may hold values from 0.5 to 2
- span_speed: float32 [64], P('pitch'), may hold values from 0.5 to 2.5
- span_filter: float32 [512], replicated, may hold values from 0.25 to 1
Outputs:
- advanced: float32 [64, 64, 1024], P('stream', 'pitch')
All inputs are finite; a program needn't handle non-finite values.
Results may differ from a plain program's by a relative error of at most 0.00008.
Values sent between devices are 32-bit elements; how exact they have to be, the bound alone decides.
A program may use at most 128 MiB of HBM per device.

v0:
```python
import math

import jax
import jax.numpy as jnp
import numpy as np
from jax import lax
from jax.experimental import pallas as pl
from jax.experimental.pallas import tpu as pltpu
from jax.sharding import PartitionSpec as P

time_step = 0.25


def spread(shard, axis, root):
    mine = lax.axis_index(axis) == root
    return lax.psum(jnp.where(mine, shard, jnp.zeros_like(shard)), axis)


def with_halo(shard, sides, width):
    for axis, dim in sides:
        peers, length = (lax.axis_size(axis), shard.shape[dim])
        up = [(i, (i + 1) % peers) for i in range(peers)]
        down = [(j, i) for i, j in up]
        last = lax.slice_in_dim(shard, length - width, length, axis=dim)
        initial = lax.slice_in_dim(shard, 0, width, axis=dim)
        before = lax.ppermute(last, axis, up)
        after = lax.ppermute(initial, axis, down)
        shard = jnp.concatenate([before, shard, after], axis=dim)
    return shard


def pitch_second(padded):
    return (
        -padded[:, 0:-4]
        + 16.0 * padded[:, 1:-3]
        - 30.0 * padded[:, 2:-2]
        + 16.0 * padded[:, 3:-1]
        - padded[:, 4:]
    ) / 12.0


def shards(
    velocity, eddy_visc, stream_op, inlet_col, planes, record, convection, span_speed, span_filter
):
    cells_x, cells_y, span_len = velocity.shape
    stream_len = stream_op.shape[0]
    span_piece = span_len // lax.axis_size("stream")
    position = lax.axis_index("stream")
    half = span_len // 2
    rows_index = lax.iota(jnp.int32, span_len)[:, None]
    mode_index = lax.iota(jnp.int32, half)[None, :]
    angle = (rows_index * mode_index % span_len).astype(jnp.float32) * (2.0 * math.pi / span_len)
    table_dft = jnp.concatenate([jnp.cos(angle), jnp.sin(angle)], axis=1)
    gains = span_filter * lax.iota(jnp.float32, half) / half
    conv_rows = convection[None, :, None]
    span_rows = span_speed[None, :, None]

    def inlet_at(section):
        whole = spread(planes[0], "stream", record[section])
        return lax.dynamic_slice_in_dim(whole, position * span_piece, span_piece, 1)

    def span_part(state):
        flat = state.reshape(-1, span_len)
        coeffs = jnp.dot(
            flat, table_dft, precision=lax.Precision.HIGHEST, preferred_element_type=jnp.float32
        )
        mixed = jnp.concatenate([coeffs[:, half:] * gains, -coeffs[:, :half] * gains], axis=1)
        back = lax.dot_general(
            mixed,
            table_dft,
            (((1,), (1,)), ((), ())),
            precision=lax.Precision.HIGHEST,
            preferred_element_type=jnp.float32,
        )
        return (back * (2.0 / span_len)).reshape(state.shape)

    def section_rate(state, section):
        inlet_slice = inlet_at(section)
        pencil = lax.all_to_all(state, "stream", split_axis=2, concat_axis=0, tiled=True)
        stream_deriv = jnp.dot(
            stream_op,
            pencil.reshape(stream_len, -1),
            precision=lax.Precision.HIGHEST,
            preferred_element_type=jnp.float32,
        )
        stream_deriv = (
            stream_deriv.reshape(pencil.shape) + inlet_col[:, None, None] * inlet_slice[None, :, :]
        )
        returned = lax.all_to_all(stream_deriv, "stream", split_axis=0, concat_axis=2, tiled=True)
        padded = with_halo(state, (("pitch", 1),), 2)
        local_terms = -(conv_rows + state) * returned + eddy_visc * pitch_second(padded)
        return local_terms - span_rows * span_part(state)

    first = section_rate(velocity, 0)
    second = section_rate(velocity + 0.5 * time_step * first, 1)
    third = section_rate(velocity + 0.5 * time_step * second, 2)
    fourth = section_rate(velocity + time_step * third, 3)
    return velocity + time_step / 6.0 * (first + 2.0 * second + 2.0 * third + fourth)


CHUNK = 8
PAIR = 2
MESH_ID = pl.DeviceIdType.MESH


def place_of(rank):
    spot, core = rank // 2, rank % 2
    plane, along = spot // 8, spot % 8
    along = along + plane * (7 - 2 * along)
    side = along // 4
    depth = along + side * (7 - 2 * along)
    return 2 * depth + side, 2 * plane + core


def rank_of(stream, pitch):
    depth, side, plane, core = stream // 2, stream % 2, pitch // 2, pitch % 2
    along = depth + side * (7 - 2 * depth)
    along = along + plane * (7 - 2 * along)
    return 2 * (8 * plane + along) + core


def halves(value):
    high = value.astype(jnp.bfloat16)
    return high, (value - high.astype(jnp.float32)).astype(jnp.bfloat16)


def mul(left, right):
    return jnp.dot(left, right, preferred_element_type=jnp.float32)


def ring_kernel(
    vel_hbm, eddy_hbm, op_hbm, col_hbm, plane_hbm, record_hbm, conv_hbm, speed_hbm, filter_hbm, table_hbm,
    out_ref,
    vel_ref, eddy_ref, op_ref, inlet_ref, plane_ref, record_ref, conv_ref, speed_ref, filter_ref, table_ref,
    in_sems, col_ref, rows_ref,
    vt, et, pt, state, eddy, inlets, row_vals, low, high, total, dx, sz, weights, op_cat,
    vel_send, vel_recv, eddy_send, eddy_recv, pl_send, pl_recv, row_send, row_recv,
    low_send, low_recv, high_send, high_recv, out_send, out_recv,
):
    me_s, me_p = lax.axis_index("stream"), lax.axis_index("pitch")
    me = rank_of(me_s, me_p)
    home = me // 8
    offset = me % 8
    above = place_of((me + 1) % 32)
    below = place_of((me + 31) % 32)
    partner = (me_s, me_p + 1 - 2 * (me_p % 2))
    core = me_p % 2

    loads = [
        pltpu.make_async_copy(source, target, in_sems.at[i])
        for i, (source, target) in enumerate(
            (
                (vel_hbm, vel_ref), (plane_hbm, plane_ref), (conv_hbm, conv_ref), (speed_hbm, speed_ref),
                (eddy_hbm, eddy_ref), (filter_hbm, filter_ref), (table_hbm, table_ref), (op_hbm, op_ref),
                (col_hbm, inlet_ref), (record_hbm, record_ref),
            )
        )
    ]
    for load in loads:
        load.start()

    barrier = pltpu.get_barrier_semaphore()

    @pl.loop(1, 32)
    def _(step):
        other = (me_s * 4 + me_p + step) % 32
        pl.semaphore_signal(barrier, inc=1, device_id=(other // 4, other % 4), device_id_type=MESH_ID)

    def rows8(index):
        return pl.ds(pl.multiple_of(index * CHUNK, CHUNK), CHUNK)

    def out_copy(src, dst, send, recv, device):
        return pltpu.make_async_remote_copy(
            src_ref=src, dst_ref=dst, send_sem=send, recv_sem=recv, device_id=device,
            device_id_type=MESH_ID,
        )

    def spread_copy(kind, j):
        src, dst, send, recv = {
            "vel": (vt, state.at[0], vel_send, vel_recv),
            "eddy": (et, eddy, eddy_send, eddy_recv),
            "plane": (pt, inlets, pl_send, pl_recv),
        }[kind]
        source = src.at[pl.ds(PAIR * j, PAIR)]
        target = dst.at[me_s] if kind == "plane" else dst.at[:, rows8(me_s)]
        rank = 8 * me_p + j
        return (
            rank,
            out_copy(source, target, send.at[j], recv.at[me_s], place_of(rank)),
            lambda: pltpu.make_async_copy(source, target, recv.at[me_s]),
        )

    def spread_start(kind, j):
        rank, remote, local = spread_copy(kind, j)

        @pl.when(rank != me)
        def _():
            remote.start()

        @pl.when(rank == me)
        def _():
            local().start()

    def spread_sent(kind):
        @pl.loop(0, 8)
        def _(j):
            rank, remote, _local = spread_copy(kind, j)

            @pl.when(rank != me)
            def _():
                remote.wait_send()

    def spread_arrived(kind, s):
        src, dst, send, recv = {
            "vel": (vt, state.at[0], vel_send, vel_recv),
            "eddy": (et, eddy, eddy_send, eddy_recv),
            "plane": (pt, inlets, pl_send, pl_recv),
        }[kind]
        target = dst.at[s] if kind == "plane" else dst.at[:, rows8(s)]
        pltpu.make_async_copy(src.at[pl.ds(0, PAIR)], target, recv.at[s]).wait()

    def low_copy(n, c):
        return out_copy(
            state.at[n, :, rows8(c)], low.at[n, :, rows8(c)], low_send.at[n, c], low_recv.at[n, c], above
        )

    def high_copy(n, c):
        return out_copy(
            state.at[n, :, rows8(c)], high.at[n, :, rows8(c)], high_send.at[n, c], high_recv.at[n, c],
            below,
        )

    def result_copy(s):
        source = state.at[4, :, rows8(s)]
        target = out_ref.at[pl.ds(PAIR * offset, PAIR)]
        return (
            out_copy(source, target, out_send.at[s], out_recv.at[offset], (s, home)),
            lambda: pltpu.make_async_copy(source, target, out_recv.at[offset]),
        )

    loads[0].wait()

    pl.semaphore_wait(barrier, 31)

    @pl.loop(0, 8)
    def _(i):
        j = (i + me_s + 1) % 8
        for y in range(PAIR):
            vt[PAIR * j + y] = jnp.squeeze(vel_ref[:, pl.ds(PAIR * j + y, 1), :], axis=1)
        spread_start("vel", j)

    def column_of(row):
        count = row.shape[1]
        own = lax.broadcasted_iota(jnp.int32, (count, count), 0) == lax.broadcasted_iota(
            jnp.int32, (count, count), 1
        )
        picked = jnp.sum(jnp.where(own, jnp.broadcast_to(row, (count, count)), 0.0), axis=1, keepdims=True)
        return jnp.broadcast_to(picked, (count, 128))

    for load in loads[1:4]:
        load.wait()
    rows_ref[0] = column_of(conv_ref[...])
    rows_ref[1] = column_of(speed_ref[...])
    for part in range(8):
        pt_part = plane_ref[0, :, 128 * part : 128 * part + 128]
        for y in range(16):
            pt[y, part : part + 1, :] = pt_part[y : y + 1, :]

    row_copy = out_copy(rows_ref, row_vals.at[core], row_send, row_recv, partner)
    row_copy.start()
    row_vals[core] = rows_ref[...]

    @pl.loop(0, 8)
    def _(i):
        spread_start("plane", (i + me_s + 1) % 8)

    for load in loads[4:]:
        load.wait()
    kernel_row = jnp.dot(
        jnp.broadcast_to(filter_ref[...], (8, 512)), table_ref[...],
        precision=lax.Precision.HIGHEST, preferred_element_type=jnp.float32,
    )[0:1]
    rolled = pltpu.roll(jnp.broadcast_to(kernel_row, (256, 1024)), 0, 1, stride=1, stride_axis=0)
    b0, b1, b2, b3 = (rolled[:, 256 * i : 256 * i + 256] for i in range(4))
    for i, block in enumerate(
        (
            0.25 * ((b0 + b2) + (b1 + b3)),
            0.25 * ((b0 + b2) - (b1 + b3)),
            0.5 * (b0 - b2),
            0.5 * (b1 - b3),
        )
    ):
        weights[0, i], weights[1, i] = halves(block)
    op_parts = halves(op_ref[...])
    source_index = lax.broadcasted_iota(jnp.int32, (64, 192), 0)
    column = lax.broadcasted_iota(jnp.int32, (64, 192), 1)
    into_high = ((column % 64 == source_index) & (column < 128)).astype(jnp.bfloat16)
    into_low = ((column % 64 == source_index) & (column >= 128)).astype(jnp.bfloat16)
    op_cat[...] = (mul(op_parts[0], into_high) + mul(op_parts[1], into_low)).astype(jnp.bfloat16)
    col_ref[...] = column_of(inlet_ref[...])

    @pl.loop(0, 8)
    def _(i):
        c = (offset + 7 - i) % 8
        spread_arrived("vel", c)
        low_copy(0, c).start()
        high_copy(0, c).start()
        j = (i + me_s + 1) % 8
        for y in range(PAIR):
            et[PAIR * j + y] = jnp.squeeze(eddy_ref[:, pl.ds(PAIR * j + y, 1), :], axis=1)
        spread_start("eddy", j)

    def products(n):
        for y in range(PAIR):
            up, down = halves(state[n, y])
            dx[y] = mul(op_cat[...], jnp.concatenate([up, down, up], axis=0))
        u = state[n].reshape(128, 1024)
        v0, v1, v2, v3 = (u[:, 256 * i : 256 * i + 256] for i in range(4))
        even, odd = v0 + v2, v1 + v3

        def times(value, *which):
            up, down = halves(value)
            count = value.shape[0]
            both = jnp.concatenate([up, down], axis=0)
            found = []
            for i in which:
                wide = mul(both, weights[0, i])
                found.append(wide[:count] + wide[count:] + mul(up, weights[1, i]))
            return found

        (first,) = times(even + odd, 0)
        (second,) = times(even - odd, 1)
        straight, crossed = times(jnp.concatenate([v0 - v2, v1 - v3], axis=0), 2, 3)
        diff0 = straight[:128] - crossed[128:]
        diff1 = crossed[:128] + straight[128:]
        for i, part in enumerate(
            (
                (first + second) + diff0,
                (first - second) + diff1,
                (first + second) - diff0,
                (first - second) - diff1,
            )
        ):
            sz[:, :, 256 * i : 256 * i + 256] = part.reshape(PAIR, 64, 256)

    source_core = home % 2

    def row_value(which, y):
        row = PAIR * offset + y
        value = row_vals[source_core, which, pl.ds(row, 1), :]
        return jnp.concatenate([jnp.broadcast_to(value, (8, 128))] * 8, axis=1)

    def combine(n):
        if n == 0:
            row_copy.wait_recv()

            @pl.loop(0, 8)
            def _(s):
                spread_arrived("plane", s)

        step = (0.5 * time_step, 0.5 * time_step, time_step, 0.0)[n]
        share = time_step / 6.0 * (1.0, 2.0, 2.0, 1.0)[n]
        gusts = []
        for y in range(PAIR):
            tile = inlets[record_ref[n], y]
            gusts.append(
                jnp.concatenate(
                    [jnp.broadcast_to(tile[i : i + 1], (8, 128)) for i in range(8)], axis=1
                )
            )
        conv = [row_value(0, y) for y in range(PAIR)]
        speed = [row_value(1, y) for y in range(PAIR)]

        @pl.loop(0, 8)
        def _(c):
            if n == 0:
                spread_arrived("eddy", c)
            low_copy(n, c).wait_recv()
            high_copy(n, c).wait_recv()
            r = rows8(c)
            column = jnp.concatenate([col_ref[r, :]] * 8, axis=1)
            rows = [low[n, 0, r], low[n, 1, r], state[n, 0, r], state[n, 1, r], high[n, 0, r], high[n, 1, r]]
            for y in range(PAIR):
                u = rows[y + 2]
                second = (
                    16.0 * (rows[y + 1] + rows[y + 3]) - (rows[y] + rows[y + 4]) - 30.0 * u
                ) * (1.0 / 12.0)
                rate = (
                    eddy[y, r] * second
                    - (conv[y] + u) * (dx[y, r] + column * gusts[y])
                    - speed[y] * sz[y, r]
                )
                if n == 0:
                    total[y, r] = u + share * rate
                    state[1, y, r] = u + step * rate
                elif n < 3:
                    total[y, r] += share * rate
                    state[n + 1, y, r] = state[0, y, r] + step * rate
                else:
                    state[4, y, r] = total[y, r] + share * rate
            if n < 3:
                low_copy(n + 1, c).start()
                high_copy(n + 1, c).start()
            else:
                remote, local = result_copy(c)
                mine = (c == me_s) & (home == me_p)

                @pl.when(jnp.logical_not(mine))
                def _():
                    remote.start()

                @pl.when(mine)
                def _():
                    local().start()

    for n in range(4):
        products(n)
        combine(n)

    spread_sent("vel")
    spread_sent("plane")
    spread_sent("eddy")
    row_copy.wait_send()

    @pl.loop(0, 8)
    def _(c):
        for n in range(4):
            low_copy(n, c).wait_send()
            high_copy(n, c).wait_send()
        mine = (c == me_s) & (home == me_p)

        @pl.when(jnp.logical_not(mine))
        def _():
            result_copy(c)[0].wait_send()

        pltpu.make_async_copy(
            state.at[4, :, rows8(0)], out_ref.at[pl.ds(PAIR * c, PAIR)], out_recv.at[c]
        ).wait()


def ring_shards(
    velocity, eddy_visc, stream_op, inlet_col, planes, record, convection, span_speed, span_filter
):
    span_len = velocity.shape[2]
    half = span_len // 2
    modes = np.arange(half)[:, None]
    angle = (modes * np.arange(span_len)[None, :] % span_len) * (2.0 * np.pi / span_len)
    table = (-2.0 / span_len * modes / half * np.sin(angle)).astype(np.float32)
    f32, dma = jnp.float32, pltpu.SemaphoreType.DMA
    result = pl.pallas_call(
        ring_kernel,
        out_shape=pltpu.VMEM((16, 8, 1024), f32),
        in_specs=[pl.BlockSpec(memory_space=pltpu.HBM)] * 10,
        out_specs=pl.BlockSpec(memory_space=pltpu.VMEM),
        scratch_shapes=[
            pltpu.VMEM((8, 16, 1024), f32),
            pltpu.VMEM((8, 16, 1024), f32),
            pltpu.VMEM((64, 64), f32),
            pltpu.VMEM((1, 64), f32),
            pltpu.VMEM((1, 16, 1024), f32),
            pltpu.SMEM((4,), jnp.int32),
            pltpu.VMEM((1, 16), f32),
            pltpu.VMEM((1, 16), f32),
            pltpu.VMEM((1, 512), f32),
            pltpu.VMEM((512, 1024), f32),
            dma((10,)),
            pltpu.VMEM((64, 128), f32),
            pltpu.VMEM((2, 16, 128), f32),
            pltpu.VMEM((16, 8, 1024), f32),
            pltpu.VMEM((16, 8, 1024), f32),
            pltpu.VMEM((16, 8, 128), f32),
            pltpu.VMEM((5, 2, 64, 1024), f32),
            pltpu.VMEM((2, 64, 1024), f32),
            pltpu.VMEM((8, 2, 8, 128), f32),
            pltpu.VMEM((2, 2, 16, 128), f32),
            pltpu.VMEM((4, 2, 64, 1024), f32),
            pltpu.VMEM((4, 2, 64, 1024), f32),
            pltpu.VMEM((2, 64, 1024), f32),
            pltpu.VMEM((2, 64, 1024), f32),
            pltpu.VMEM((2, 64, 1024), f32),
            pltpu.VMEM((2, 4, 256, 256), jnp.bfloat16),
            pltpu.VMEM((64, 192), jnp.bfloat16),
            dma((8,)), dma((8,)), dma((8,)), dma((8,)), dma((8,)), dma((8,)), dma, dma,
            dma((4, 8)), dma((4, 8)), dma((4, 8)), dma((4, 8)), dma((8,)), dma((8,)),
        ],
        compiler_params=pltpu.CompilerParams(
            collective_id=0, has_side_effects=True, vmem_limit_bytes=56 * 2**20
        ),
    )(
        velocity,
        eddy_visc,
        stream_op,
        inlet_col[None, :],
        planes,
        record,
        convection[None, :],
        span_speed[None, :],
        span_filter[None, :],
        jnp.asarray(table),
    )
    return result.transpose(1, 0, 2)


def either(velocity, *others):
    fits = (
        lax.axis_size("stream") == 8
        and lax.axis_size("pitch") == 4
        and velocity.shape == (8, 16, 1024)
    )
    return (ring_shards if fits else shards)(velocity, *others)


def solution(mesh):
    placed = (
        P("stream", "pitch", None),
        P("stream", "pitch", None),
        P(),
        P(),
        P("stream", "pitch", None),
        P(),
        P("pitch"),
        P("pitch"),
        P(),
    )
    return jax.shard_map(
        either, mesh=mesh, in_specs=placed, out_specs=P("stream", "pitch", None), check_vma=False
    )
```

profile of v0, /device:TPU:0, one launch (start us, length us, event | category | flops | bytes accessed | tf_op | source)
XLA Modules:
  0.0 67.5 jit_solution(6597464930947199605)
XLA Ops:
  0.0 66.3 %shard_map.100 = f32[16,8,1024]{2,1,0:T(8,128)S(1)} custom-call(f32[8,16,1024]{2,1,0:T(8,128)} %vel_hbm.1, f32[8,16,1024]{2,1,0:T(8,128)} %eddy_hbm.1, f32[64,64]{1,0:T(8,128)} %op_hbm.1, f32[1,64]{1,0:T(1,128)} %bitcast.7, f32[1,16,1024]{2,1,0:T(8,128)} %plane_hbm.1, s32[4]{0:T(128)} %record_hbm.1, f32[1,16]{1,0:T(1,128)} %bitcast.8, f32[1,16]{1,0:T(1,128)} %bitcast.9, ...), custom_call_target="tpu_custom_call" | custom-call | tf_op jit(solution)/shard_map/pallas_call | solution.py:450
  66.4 1.1 %copy.11 = f32[8,16,1024]{2,1,0:T(8,128)} copy(f32[8,16,1024]{2,0,1:T(8,128)S(1)} %bitcast.5) | data formatting | bytes 1048576 | tf_op jit(solution)/shard_map/transpose | solution.py:501
where the time goes:
time: 68.1 us; the launch traced here: 67.5 us
  Pallas kernels  66.3 us (97%)
  local copies, waits for them, and re-layouts  1.1 us (2%)
    pallas_call x1, Pallas kernels, ring_shards(): pl.pallas_call(ring_kernel, out_shape=pltpu.VMEM((16, 8, 1024), f32), in_...  66.3 us

commit v1 on v0

--- a/solution.py
+++ b/solution.py
@@ -104,19 +104,19 @@
 
 
 def place_of(rank):
-    spot, core = rank // 2, rank % 2
-    plane, along = spot // 8, spot % 8
-    along = along + plane * (7 - 2 * along)
-    side = along // 4
-    depth = along + side * (7 - 2 * along)
-    return 2 * depth + side, 2 * plane + core
+    spot, turn = rank // 2, rank % 2
+    plane, step = spot // 8, spot % 8
+    along = step + plane * (7 - 2 * step)
+    depth = along // 2
+    core = (plane + depth // 2 + step + turn) % 2
+    return 2 * depth + (along + 1) // 2 % 2, 2 * plane + core
 
 
 def rank_of(stream, pitch):
     depth, side, plane, core = stream // 2, stream % 2, pitch // 2, pitch % 2
-    along = depth + side * (7 - 2 * depth)
-    along = along + plane * (7 - 2 * along)
-    return 2 * (8 * plane + along) + core
+    along = 2 * depth + (side + depth) % 2
+    step = along + plane * (7 - 2 * along)
+    return 2 * (8 * plane + step) + (core + plane + depth // 2 + step) % 2
 
 
 def halves(value):
@@ -136,6 +136,7 @@
     vt, et, pt, state, eddy, inlets, row_vals, low, high, total, dx, sz, weights, op_cat,
     vel_send, vel_recv, eddy_send, eddy_recv, pl_send, pl_recv, row_send, row_recv,
     low_send, low_recv, high_send, high_recv, out_send, out_recv,
+    eddy_via, eddy_via_recv, eddy_on, edge_send,
 ):
     me_s, me_p = lax.axis_index("stream"), lax.axis_index("pitch")
     me = rank_of(me_s, me_p)
@@ -145,6 +146,24 @@
     below = place_of((me + 31) % 32)
     partner = (me_s, me_p + 1 - 2 * (me_p % 2))
     core = me_p % 2
+    upper = me_s // 4
+    group_upper = (me_p + 1) // 2 % 2
+    feeds = (me_s == 2) | (me_s == 4)
+    relays = (me_s == 3) | (me_s == 5)
+    feeds_in = feeds & (group_upper != upper)
+    relays_in = relays & (group_upper == upper)
+    crossing = group_upper != upper
+    mirrored = (me_s + 2 * (1 - upper)) % 4
+    first_vel = jnp.where(crossing & (mirrored < 2), 6, 2)
+    first_eddy = jnp.where(crossing & (mirrored == 1), 6, 2)
+    edge = 7 * (1 - core)
+    edge_peer = place_of((8 * me_p + edge + 33 - 2 * core) % 32)
+    ends_low, ends_high = me % 16 == 7, me % 16 == 8
+    inner = (offset >= 2) & (offset <= 5)
+
+    def arrival(i):
+        turn = jnp.where(inner, 7 - i % 4, 4 + i % 4)
+        return jnp.where(i < 4, 4 * upper + i % 4, jnp.where(upper == 1, (turn + 2) % 4, turn))
 
     loads = [
         pltpu.make_async_copy(source, target, in_sems.at[i])
@@ -156,7 +175,7 @@
             )
         )
     ]
-    for load in loads:
+    for load in loads[:4]:
         load.start()
 
     barrier = pltpu.get_barrier_semaphore()
@@ -193,13 +212,57 @@
     def spread_start(kind, j):
         rank, remote, local = spread_copy(kind, j)
 
-        @pl.when(rank != me)
+        via = feeds_in & (j >= 2) & (j <= 5) if kind == "eddy" else False
+
+        @pl.when((rank != me) & jnp.logical_not(via))
         def _():
             remote.start()
 
         @pl.when(rank == me)
         def _():
             local().start()
+
+        if kind == "eddy":
+
+            @pl.when(via)
+            def _():
+                k = (j + 6) % 8
+                out_copy(
+                    et.at[pl.ds(PAIR * j, PAIR)], eddy_via.at[k], eddy_send.at[j], eddy_via_recv.at[k],
+                    (me_s + 1, me_p + 1 - 2 * core),
+                ).start()
+
+    def forward_eddy(k):
+        source = (me_s + 7) % 8
+        return (
+            pltpu.make_async_copy(eddy_via.at[k], eddy_via.at[k], eddy_via_recv.at[k]),
+            out_copy(
+                eddy_via.at[k], eddy.at[:, rows8(source)], eddy_on.at[k], eddy_recv.at[source],
+                place_of(8 * (me_p + 1 - 2 * core) + 2 + k),
+            ),
+        )
+
+    def edge_copy(to_low):
+        dst, recv = (low, low_recv) if to_low else (high, high_recv)
+        return out_copy(
+            vt.at[pl.ds(PAIR * edge, PAIR)], dst.at[0, :, rows8(me_s)], edge_send, recv.at[0, me_s],
+            edge_peer,
+        )
+
+    def edge_start(j):
+        @pl.when(crossing & (j == edge) & (core == 0))
+        def _():
+            edge_copy(True).start()
+
+        @pl.when(crossing & (j == edge) & (core == 1))
+        def _():
+            edge_copy(False).start()
+
+    def low_sends(n, c):
+        return jnp.logical_not(ends_low & (c // 4 != upper)) if n == 0 else True
+
+    def high_sends(n, c):
+        return jnp.logical_not(ends_high & (c // 4 != upper)) if n == 0 else True
 
     def spread_sent(kind):
         @pl.loop(0, 8)
@@ -239,15 +302,18 @@
         )
 
     loads[0].wait()
+    for load in loads[4:]:
+        load.start()
 
     pl.semaphore_wait(barrier, 31)
 
     @pl.loop(0, 8)
     def _(i):
-        j = (i + me_s + 1) % 8
+        j = (i + first_vel) % 8
         for y in range(PAIR):
             vt[PAIR * j + y] = jnp.squeeze(vel_ref[:, pl.ds(PAIR * j + y, 1), :], axis=1)
         spread_start("vel", j)
+        edge_start(j)
 
     def column_of(row):
         count = row.shape[1]
@@ -301,14 +367,29 @@
 
     @pl.loop(0, 8)
     def _(i):
-        c = (offset + 7 - i) % 8
+        c = arrival(i)
         spread_arrived("vel", c)
-        low_copy(0, c).start()
-        high_copy(0, c).start()
-        j = (i + me_s + 1) % 8
+
+        @pl.when(low_sends(0, c))
+        def _():
+            low_copy(0, c).start()
+
+        @pl.when(high_sends(0, c))
+        def _():
+            high_copy(0, c).start()
+
+        j = (i + first_eddy) % 8
         for y in range(PAIR):
             et[PAIR * j + y] = jnp.squeeze(eddy_ref[:, pl.ds(PAIR * j + y, 1), :], axis=1)
         spread_start("eddy", j)
+
+    @pl.when(relays_in)
+    def _():
+        @pl.loop(0, 4)
+        def _(k):
+            arrived, onward = forward_eddy(k)
+            arrived.wait()
+            onward.start()
 
     def products(n):
         for y in range(PAIR):
@@ -372,7 +453,8 @@
         speed = [row_value(1, y) for y in range(PAIR)]
 
         @pl.loop(0, 8)
-        def _(c):
+        def _(i):
+            c = arrival(i) if n == 0 else i
             if n == 0:
                 spread_arrived("eddy", c)
             low_copy(n, c).wait_recv()
@@ -417,6 +499,15 @@
         products(n)
         combine(n)
 
+    @pl.when(relays_in)
+    def _():
+        for k in range(4):
+            forward_eddy(k)[1].wait_send()
+
+    @pl.when(crossing)
+    def _():
+        edge_copy(True).wait_send()
+
     spread_sent("vel")
     spread_sent("plane")
     spread_sent("eddy")
@@ -425,8 +516,15 @@
     @pl.loop(0, 8)
     def _(c):
         for n in range(4):
-            low_copy(n, c).wait_send()
-            high_copy(n, c).wait_send()
+
+            @pl.when(low_sends(n, c))
+            def _():
+                low_copy(n, c).wait_send()
+
+            @pl.when(high_sends(n, c))
+            def _():
+                high_copy(n, c).wait_send()
+
         mine = (c == me_s) & (home == me_p)
 
         @pl.when(jnp.logical_not(mine))
@@ -482,6 +580,7 @@
             pltpu.VMEM((64, 192), jnp.bfloat16),
             dma((8,)), dma((8,)), dma((8,)), dma((8,)), dma((8,)), dma((8,)), dma, dma,
             dma((4, 8)), dma((4, 8)), dma((4, 8)), dma((4, 8)), dma((8,)), dma((8,)),
+            pltpu.VMEM((4, 2, 8, 1024), f32), dma((4,)), dma((4,)), dma,
         ],
         compiler_params=pltpu.CompilerParams(
             collective_id=0, has_side_effects=True, vmem_limit_bytes=56 * 2**20

time: 68.1 us -> 64 us (0.940)
  Pallas kernels: 66.3 us -> 62.7 us
    pallas_call x1, Pallas kernels: 66.3 us -> 62.7 us  [ring_shards(): pl.pallas_call(ring_kernel, out_shape=pltpu.VMEM((16, 8, 1024), f32), in_...]
where the time goes in v1:
time: 64 us; the launch traced here: 63.8 us
  Pallas kernels  62.7 us (98%)
  local copies, waits for them, and re-layouts  1.1 us (2%)
    pallas_call x1, Pallas kernels, ring_shards(): pl.pallas_call(ring_kernel, out_shape=pltpu.VMEM((16, 8, 1024), f32), in_...  62.7 us

profile of v1, /device:TPU:0, one launch (start us, length us, event | category | flops | bytes accessed | tf_op | source)
XLA Modules:
  0.0 63.8 jit_solution(13990790484659903369)
XLA Ops:
  0.0 62.7 %shard_map.100 = f32[16,8,1024]{2,1,0:T(8,128)S(1)} custom-call(f32[8,16,1024]{2,1,0:T(8,128)} %vel_hbm.1, f32[8,16,1024]{2,1,0:T(8,128)} %eddy_hbm.1, f32[64,64]{1,0:T(8,128)} %op_hbm.1, f32[1,64]{1,0:T(1,128)} %bitcast.7, f32[1,16,1024]{2,1,0:T(8,128)} %plane_hbm.1, s32[4]{0:T(128)} %record_hbm.1, f32[1,16]{1,0:T(1,128)} %bitcast.8, f32[1,16]{1,0:T(1,128)} %bitcast.9, ...), custom_call_target="tpu_custom_call" | custom-call | tf_op jit(solution)/shard_map/pallas_call | solution.py:548
  62.7 1.1 %copy.11 = f32[8,16,1024]{2,1,0:T(8,128)} copy(f32[8,16,1024]{2,0,1:T(8,128)S(1)} %bitcast.5) | data formatting | bytes 1048576 | tf_op jit(solution)/shard_map/transpose | solution.py:600

commit v2 on v1

--- a/solution.py
+++ b/solution.py
@@ -136,7 +136,7 @@
     vt, et, pt, state, eddy, inlets, row_vals, low, high, total, dx, sz, weights, op_cat,
     vel_send, vel_recv, eddy_send, eddy_recv, pl_send, pl_recv, row_send, row_recv,
     low_send, low_recv, high_send, high_recv, out_send, out_recv,
-    eddy_via, eddy_via_recv, eddy_on, edge_send,
+    eddy_via, eddy_via_recv, eddy_on, edge_send, landed,
 ):
     me_s, me_p = lax.axis_index("stream"), lax.axis_index("pitch")
     me = rank_of(me_s, me_p)
@@ -295,7 +295,7 @@
 
     def result_copy(s):
         source = state.at[4, :, rows8(s)]
-        target = out_ref.at[pl.ds(PAIR * offset, PAIR)]
+        target = landed.at[pl.ds(PAIR * offset, PAIR)]
         return (
             out_copy(source, target, out_send.at[s], out_recv.at[offset], (s, home)),
             lambda: pltpu.make_async_copy(source, target, out_recv.at[offset]),
@@ -532,8 +532,10 @@
             result_copy(c)[0].wait_send()
 
         pltpu.make_async_copy(
-            state.at[4, :, rows8(0)], out_ref.at[pl.ds(PAIR * c, PAIR)], out_recv.at[c]
+            state.at[4, :, rows8(0)], landed.at[pl.ds(PAIR * c, PAIR)], out_recv.at[c]
         ).wait()
+        for y in range(PAIR):
+            out_ref[:, pl.ds(PAIR * c + y, 1), :] = jnp.expand_dims(landed[PAIR * c + y], 1)
 
 
 def ring_shards(
@@ -547,7 +549,7 @@
     f32, dma = jnp.float32, pltpu.SemaphoreType.DMA
     result = pl.pallas_call(
         ring_kernel,
-        out_shape=pltpu.VMEM((16, 8, 1024), f32),
+        out_shape=pltpu.VMEM((8, 16, 1024), f32),
         in_specs=[pl.BlockSpec(memory_space=pltpu.HBM)] * 10,
         out_specs=pl.BlockSpec(memory_space=pltpu.VMEM),
         scratch_shapes=[
@@ -581,6 +583,7 @@
             dma((8,)), dma((8,)), dma((8,)), dma((8,)), dma((8,)), dma((8,)), dma, dma,
             dma((4, 8)), dma((4, 8)), dma((4, 8)), dma((4, 8)), dma((8,)), dma((8,)),
             pltpu.VMEM((4, 2, 8, 1024), f32), dma((4,)), dma((4,)), dma,
+            pltpu.VMEM((16, 8, 1024), f32),
         ],
         compiler_params=pltpu.CompilerParams(
             collective_id=0, has_side_effects=True, vmem_limit_bytes=56 * 2**20
@@ -597,7 +600,7 @@
         span_filter[None, :],
         jnp.asarray(table),
     )
-    return result.transpose(1, 0, 2)
+    return result
 
 
 def either(velocity, *others):

time: 64 us -> 63.8 us (level)
    transpose x1 -> x0, local copies, waits for them, and re-layouts: 1.1 us -> none  [ring_shards(): return result.transpose(1, 0, 2)]
    unnamed x0 -> x1, local copies, waits for them, and re-layouts: none -> 0.8 us
where the time goes in v2:
time: 63.8 us; the launch traced here: 63.6 us
  Pallas kernels  62.8 us (98%)
  local copies, waits for them, and re-layouts  0.8 us (1%)
    pallas_call x1, Pallas kernels, ring_shards(): pl.pallas_call(ring_kernel, out_shape=pltpu.VMEM((8, 16, 1024), f32), in_...  62.8 us

profile of v2, /device:TPU:0, one launch (start us, length us, event | category | flops | bytes accessed | tf_op | source)
XLA Modules:
  0.0 63.6 jit_solution(9697642091271013798)
XLA Ops:
  0.0 62.8 %shard_map.100 = f32[8,16,1024]{2,1,0:T(8,128)S(1)} custom-call(f32[8,16,1024]{2,1,0:T(8,128)} %vel_hbm.1, f32[8,16,1024]{2,1,0:T(8,128)} %eddy_hbm.1, f32[64,64]{1,0:T(8,128)} %op_hbm.1, f32[1,64]{1,0:T(1,128)} %bitcast.5, f32[1,16,1024]{2,1,0:T(8,128)} %plane_hbm.1, s32[4]{0:T(128)} %record_hbm.1, f32[1,16]{1,0:T(1,128)} %bitcast.6, f32[1,16]{1,0:T(1,128)} %bitcast.7, ...), custom_call_target="tpu_custom_call" | custom-call | tf_op jit(solution)/shard_map/pallas_call | solution.py:550
  62.8 0.8 %copy.12 = f32[8,16,1024]{2,1,0:T(8,128)} copy(f32[8,16,1024]{2,1,0:T(8,128)S(1)} %shard_map.100) | data formatting | bytes 1048576

commit v3 on v2

--- a/solution.py
+++ b/solution.py
@@ -106,17 +106,17 @@
 def place_of(rank):
     spot, turn = rank // 2, rank % 2
     plane, step = spot // 8, spot % 8
-    along = step + plane * (7 - 2 * step)
+    along = step + (1 - plane) * (7 - 2 * step)
     depth = along // 2
-    core = (plane + depth // 2 + step + turn) % 2
+    core = (plane + depth // 2 + step + turn + 1) % 2
     return 2 * depth + (along + 1) // 2 % 2, 2 * plane + core
 
 
 def rank_of(stream, pitch):
     depth, side, plane, core = stream // 2, stream % 2, pitch // 2, pitch % 2
     along = 2 * depth + (side + depth) % 2
-    step = along + plane * (7 - 2 * along)
-    return 2 * (8 * plane + step) + (core + plane + depth // 2 + step) % 2
+    step = along + (1 - plane) * (7 - 2 * along)
+    return 2 * (8 * plane + step) + (core + plane + depth // 2 + step + 1) % 2
 
 
 def halves(value):
@@ -147,7 +147,7 @@
     partner = (me_s, me_p + 1 - 2 * (me_p % 2))
     core = me_p % 2
     upper = me_s // 4
-    group_upper = (me_p + 1) // 2 % 2
+    group_upper = 1 - (me_p + 1) // 2 % 2
     feeds = (me_s == 2) | (me_s == 4)
     relays = (me_s == 3) | (me_s == 5)
     feeds_in = feeds & (group_upper != upper)

time: 63.8 us -> 62.9 us (0.986); the launches traced: 63.6 us -> 61.8 us
  Pallas kernels: 62.8 us -> 61 us
    pallas_call x1, Pallas kernels: 62.8 us -> 61 us  [ring_shards(): pl.pallas_call(ring_kernel, out_shape=pltpu.VMEM((8, 16, 1024), f32), in_...]
where the time goes in v3:
time: 62.9 us; the launch traced here: 61.8 us
  Pallas kernels  61 us (97%)
  local copies, waits for them, and re-layouts  0.8 us (1%)
    pallas_call x1, Pallas kernels, ring_shards(): pl.pallas_call(ring_kernel, out_shape=pltpu.VMEM((8, 16, 1024), f32), in_...  61 us

profile of v3, /device:TPU:0, one launch (start us, length us, event | category | flops | bytes accessed | tf_op | source)
XLA Modules:
  0.0 61.8 jit_solution(18255934757021140116)
XLA Ops:
  0.0 61.0 %shard_map.100 = f32[8,16,1024]{2,1,0:T(8,128)S(1)} custom-call(f32[8,16,1024]{2,1,0:T(8,128)} %vel_hbm.1, f32[8,16,1024]{2,1,0:T(8,128)} %eddy_hbm.1, f32[64,64]{1,0:T(8,128)} %op_hbm.1, f32[1,64]{1,0:T(1,128)} %bitcast.5, f32[1,16,1024]{2,1,0:T(8,128)} %plane_hbm.1, s32[4]{0:T(128)} %record_hbm.1, f32[1,16]{1,0:T(1,128)} %bitcast.6, f32[1,16]{1,0:T(1,128)} %bitcast.7, ...), custom_call_target="tpu_custom_call" | custom-call | tf_op jit(solution)/shard_map/pallas_call | solution.py:550
  61.0 0.8 %copy.12 = f32[8,16,1024]{2,1,0:T(8,128)} copy(f32[8,16,1024]{2,1,0:T(8,128)S(1)} %shard_map.100) | data formatting | bytes 1048576

commit v4 on v3

--- a/solution.py
+++ b/solution.py
@@ -367,21 +367,23 @@
 
     @pl.loop(0, 8)
     def _(i):
-        c = arrival(i)
-        spread_arrived("vel", c)
-
-        @pl.when(low_sends(0, c))
-        def _():
-            low_copy(0, c).start()
-
-        @pl.when(high_sends(0, c))
-        def _():
-            high_copy(0, c).start()
-
         j = (i + first_eddy) % 8
         for y in range(PAIR):
             et[PAIR * j + y] = jnp.squeeze(eddy_ref[:, pl.ds(PAIR * j + y, 1), :], axis=1)
         spread_start("eddy", j)
+
+    @pl.loop(0, 8)
+    def _(i):
+        c = arrival(i)
+        spread_arrived("vel", c)
+
+        @pl.when(low_sends(0, c))
+        def _():
+            low_copy(0, c).start()
+
+        @pl.when(high_sends(0, c))
+        def _():
+            high_copy(0, c).start()
 
     @pl.when(relays_in)
     def _():

time: 62.9 us -> 62.4 us (level)
  no operation moved by 1% of the time
where the time goes in v4:
time: 62.4 us; the launch traced here: 61.8 us
  Pallas kernels  61 us (98%)
  local copies, waits for them, and re-layouts  0.8 us (1%)
    pallas_call x1, Pallas kernels, ring_shards(): pl.pallas_call(ring_kernel, out_shape=pltpu.VMEM((8, 16, 1024), f32), in_...  61 us

profile of v4, /device:TPU:0, one launch (start us, length us, event | category | flops | bytes accessed | tf_op | source)
XLA Modules:
  0.0 61.8 jit_solution(14255408824755011256)
XLA Ops:
  0.0 61.0 %shard_map.100 = f32[8,16,1024]{2,1,0:T(8,128)S(1)} custom-call(f32[8,16,1024]{2,1,0:T(8,128)} %vel_hbm.1, f32[8,16,1024]{2,1,0:T(8,128)} %eddy_hbm.1, f32[64,64]{1,0:T(8,128)} %op_hbm.1, f32[1,64]{1,0:T(1,128)} %bitcast.5, f32[1,16,1024]{2,1,0:T(8,128)} %plane_hbm.1, s32[4]{0:T(128)} %record_hbm.1, f32[1,16]{1,0:T(1,128)} %bitcast.6, f32[1,16]{1,0:T(1,128)} %bitcast.7, ...), custom_call_target="tpu_custom_call" | custom-call | tf_op jit(solution)/shard_map/pallas_call | solution.py:552
  61.0 0.8 %copy.12 = f32[8,16,1024]{2,1,0:T(8,128)} copy(f32[8,16,1024]{2,1,0:T(8,128)S(1)} %shard_map.100) | data formatting | bytes 1048576

commit v5 on v4

--- a/solution.py
+++ b/solution.py
@@ -385,13 +385,13 @@
         def _():
             high_copy(0, c).start()
 
-    @pl.when(relays_in)
-    def _():
-        @pl.loop(0, 4)
-        def _(k):
-            arrived, onward = forward_eddy(k)
-            arrived.wait()
-            onward.start()
+        @pl.when(relays_in & (i == 4))
+        def _():
+            @pl.loop(0, 4)
+            def _(k):
+                arrived, onward = forward_eddy(k)
+                arrived.wait()
+                onward.start()
 
     def products(n):
         for y in range(PAIR):

time: 62.4 us -> 62.4 us (level)
  no operation moved by 1% of the time
where the time goes in v5:
time: 62.4 us; the launch traced here: 61.8 us
  Pallas kernels  61 us (98%)
  local copies, waits for them, and re-layouts  0.8 us (1%)
    pallas_call x1, Pallas kernels, ring_shards(): pl.pallas_call(ring_kernel, out_shape=pltpu.VMEM((8, 16, 1024), f32), in_...  61 us

profile of v5, /device:TPU:0, one launch (start us, length us, event | category | flops | bytes accessed | tf_op | source)
XLA Modules:
  0.0 61.8 jit_solution(2491143772998236542)
XLA Ops:
  0.0 61.0 %shard_map.100 = f32[8,16,1024]{2,1,0:T(8,128)S(1)} custom-call(f32[8,16,1024]{2,1,0:T(8,128)} %vel_hbm.1, f32[8,16,1024]{2,1,0:T(8,128)} %eddy_hbm.1, f32[64,64]{1,0:T(8,128)} %op_hbm.1, f32[1,64]{1,0:T(1,128)} %bitcast.5, f32[1,16,1024]{2,1,0:T(8,128)} %plane_hbm.1, s32[4]{0:T(128)} %record_hbm.1, f32[1,16]{1,0:T(1,128)} %bitcast.6, f32[1,16]{1,0:T(1,128)} %bitcast.7, ...), custom_call_target="tpu_custom_call" | custom-call | tf_op jit(solution)/shard_map/pallas_call | solution.py:552
  61.0 0.8 %copy.12 = f32[8,16,1024]{2,1,0:T(8,128)} copy(f32[8,16,1024]{2,1,0:T(8,128)S(1)} %shard_map.100) | data formatting | bytes 1048576

commit v6 on v5

--- a/solution.py
+++ b/solution.py
@@ -385,7 +385,7 @@
         def _():
             high_copy(0, c).start()
 
-        @pl.when(relays_in & (i == 4))
+        @pl.when(relays_in & (i == 2))
         def _():
             @pl.loop(0, 4)
             def _(k):

time: 62.4 us -> 62.4 us (level)
  no operation moved by 1% of the time
where the time goes in v6:
time: 62.4 us; the launch traced here: 61.8 us
  Pallas kernels  61 us (98%)
  local copies, waits for them, and re-layouts  0.8 us (1%)
    pallas_call x1, Pallas kernels, ring_shards(): pl.pallas_call(ring_kernel, out_shape=pltpu.VMEM((8, 16, 1024), f32), in_...  61 us

profile of v6, /device:TPU:0, one launch (start us, length us, event | category | flops | bytes accessed | tf_op | source)
XLA Modules:
  0.0 61.8 jit_solution(8268108543872410180)
XLA Ops:
  0.0 61.0 %shard_map.100 = f32[8,16,1024]{2,1,0:T(8,128)S(1)} custom-call(f32[8,16,1024]{2,1,0:T(8,128)} %vel_hbm.1, f32[8,16,1024]{2,1,0:T(8,128)} %eddy_hbm.1, f32[64,64]{1,0:T(8,128)} %op_hbm.1, f32[1,64]{1,0:T(1,128)} %bitcast.5, f32[1,16,1024]{2,1,0:T(8,128)} %plane_hbm.1, s32[4]{0:T(128)} %record_hbm.1, f32[1,16]{1,0:T(1,128)} %bitcast.6, f32[1,16]{1,0:T(1,128)} %bitcast.7, ...), custom_call_target="tpu_custom_call" | custom-call | tf_op jit(solution)/shard_map/pallas_call | solution.py:552
  61.0 0.8 %copy.12 = f32[8,16,1024]{2,1,0:T(8,128)} copy(f32[8,16,1024]{2,1,0:T(8,128)S(1)} %shard_map.100) | data formatting | bytes 1048576

commit v7 on v5

--- a/solution.py
+++ b/solution.py
@@ -175,15 +175,16 @@
             )
         )
     ]
-    for load in loads[:4]:
-        load.start()
-
     barrier = pltpu.get_barrier_semaphore()
+    loads[0].start()
 
     @pl.loop(1, 32)
     def _(step):
-        other = (me_s * 4 + me_p + step) % 32
+        other = (me_s * 4 + me_p + 32 - step) % 32
         pl.semaphore_signal(barrier, inc=1, device_id=(other // 4, other % 4), device_id_type=MESH_ID)
+
+    for load in loads[1:4]:
+        load.start()
 
     def rows8(index):
         return pl.ds(pl.multiple_of(index * CHUNK, CHUNK), CHUNK)

time: 62.4 us -> 63.1 us (1.011)
  no operation moved by 1% of the time
where the time goes in v7:
time: 63.1 us; the launch traced here: 62.1 us
  Pallas kernels  61.3 us (97%)
  local copies, waits for them, and re-layouts  0.8 us (1%)
    pallas_call x1, Pallas kernels, ring_shards(): pl.pallas_call(ring_kernel, out_shape=pltpu.VMEM((8, 16, 1024), f32), in_...  61.3 us

profile of v7, /device:TPU:0, one launch (start us, length us, event | category | flops | bytes accessed | tf_op | source)
XLA Modules:
  0.0 62.1 jit_solution(14619688815827903101)
XLA Ops:
  0.0 61.3 %shard_map.100 = f32[8,16,1024]{2,1,0:T(8,128)S(1)} custom-call(f32[8,16,1024]{2,1,0:T(8,128)} %vel_hbm.1, f32[8,16,1024]{2,1,0:T(8,128)} %eddy_hbm.1, f32[64,64]{1,0:T(8,128)} %op_hbm.1, f32[1,64]{1,0:T(1,128)} %bitcast.5, f32[1,16,1024]{2,1,0:T(8,128)} %plane_hbm.1, s32[4]{0:T(128)} %record_hbm.1, f32[1,16]{1,0:T(1,128)} %bitcast.6, f32[1,16]{1,0:T(1,128)} %bitcast.7, ...), custom_call_target="tpu_custom_call" | custom-call | tf_op jit(solution)/shard_map/pallas_call | solution.py:553
  61.3 0.8 %copy.12 = f32[8,16,1024]{2,1,0:T(8,128)} copy(f32[8,16,1024]{2,1,0:T(8,128)S(1)} %shard_map.100) | data formatting | bytes 1048576
